TPU v7x, 32 devices: a whole 2x2x4 slice. The times are simulated.
32 devices in a mesh: dp: 4 (over y, x), tensor: 8 (over z, core).
Axes of the slice: x: 2, y: 2, z: 4, core: 2. Of those that a mesh axis runs over, the one named last changes fastest.
Arguments:
- real_feats: bfloat16 [2048, 1536], P(('dp', 'tensor')), may hold values from -6 to 6
- fake_feats: bfloat16 [2048, 1536], P(('dp', 'tensor')), may hold values from -6 to 6
- mix_num: int32 [2048], P(('dp', 'tensor')), may hold values from 0 to 256
- w_first: bfloat16 [1536, 12288], P(None, 'tensor'), may hold values from -0.15625 to 0.15625
- bias: float32 [12288], P('tensor'), may hold values from -3 to 3
- head: float32 [12288], P('tensor'), may hold values from -0.0546875 to 0.0546875
Outputs:
- grad_w: float32 [1536, 12288], P('dp', 'tensor')
- grad_bias: float32 [12288], P('tensor')
- grad_head: float32 [12288], P('tensor')
- penalty: float32 [], replicated
All inputs are finite; a program needn't handle non-finite values.
Results may differ from a plain program's by a relative error of at most 0.0005.
Values may be sent and summed in bfloat16 or wider, within the bound.
A program may use at most 64 MiB of HBM per device.

v0:
```python
import jax
import jax.numpy as jnp
from jax import lax
from jax.sharding import PartitionSpec as P


def row_contract(left, right):
    return lax.dot_general(
        left, right, (((0,), (0,)), ((), ())), preferred_element_type=jnp.float32
    )


def local(real_feats, fake_feats, mix_num, w_first, bias, head):
    coef = mix_num.astype(jnp.float32) / 256.0
    real_f = real_feats.astype(jnp.float32)
    mixed = (real_f + coef[:, None] * (fake_feats.astype(jnp.float32) - real_f)).astype(
        jnp.bfloat16
    )
    group = lax.all_gather(mixed, "tensor", axis=0, tiled=True)
    z = jnp.dot(group, w_first, preferred_element_type=jnp.float32) + bias
    sg = jax.nn.sigmoid(z)
    d1 = sg * (1.0 + z * (1.0 - sg))
    d2 = sg * (1.0 - sg) * (2.0 + z * (1.0 - 2.0 * sg))
    u = (d1 * head).astype(jnp.bfloat16)
    total_rows = group.shape[0] * lax.axis_size("dp")
    grad_in = lax.psum_scatter(
        lax.dot_general(
            u, w_first, (((1,), (1,)), ((), ())), preferred_element_type=jnp.float32
        ).astype(jnp.bfloat16),
        "tensor",
        scatter_dimension=0,
        tiled=True,
    ).astype(jnp.float32)
    norm = jnp.sqrt(jnp.sum(grad_in * grad_in, axis=1) + 1e-06)
    scale = 20.0 * (norm - 1.0) / norm
    scaled = (scale[:, None] * grad_in).astype(jnp.bfloat16)
    loss = lax.psum(jnp.sum((norm - 1.0) ** 2), ("dp", "tensor"))
    big = lax.all_gather(scaled, "tensor", axis=0, tiled=True)
    penalty = 10.0 * loss / total_rows
    p = jnp.dot(big, w_first, preferred_element_type=jnp.float32)
    dz = p * head * d2
    dzb = dz.astype(jnp.bfloat16)
    partial_w = row_contract(group, dzb)
    partial_w = partial_w + row_contract(big, u)
    grad_w = lax.psum_scatter(partial_w, "dp", scatter_dimension=0, tiled=True)
    grad_bias, grad_head = lax.psum((jnp.sum(dz, axis=0), jnp.sum(p * d1, axis=0)), "dp")
    return (grad_w, grad_bias, grad_head, penalty)


def solution(mesh):
    placed = (
        P(("dp", "tensor"), None),
        P(("dp", "tensor"), None),
        P(("dp", "tensor")),
        P(None, "tensor"),
        P("tensor"),
        P("tensor"),
    )
    return jax.shard_map(
        local,
        mesh=mesh,
        in_specs=placed,
        out_specs=(P("dp", "tensor"), P("tensor"), P("tensor"), P()),
        check_vma=False,
    )
```

profile of v0, /device:TPU:0, one launch (start us, length us, event | category | flops | bytes accessed | tf_op | source)
XLA Modules:
  0.0 231.7 jit_solution(5937628214392477020)
XLA Ops:
  7.2 0.0 all-gather.3.cloned.1.call-start
  7.2 0.7 convert_multiply_fusion.2
  7.9 1.8 fusion.7
  9.7 0.0 all-gather.3.cloned.1.call-update
  9.7 0.0 copy-start.2
  9.7 0.0 reduce-scatter.3.cloned.1.call-start
  9.8 28.2 %all-gather.3.cloned.1.call-done = bf16[512,1536]{1,0:T(8,128)(2,1)} async-done(((bf16[64,1536]{1,0:T(8,128)(2,1)}), bf16[512,1536]{1,0:T(8,128)(2,1)}) %all-gather.3.cloned.1.call-update) | async-done | bytes 1572880 | tf_op jit(solution)/shard_map/all_gather | solution.py:19
  38.0 5.0 %convolution_add_fusion.1 = f32[512,1536]{1,0:T(8,128)S(1)} fusion(bf16[512,1536]{1,0:T(8,128)(2,1)} %all-gather.3.cloned.1.call-done, bf16[1536,1536]{1,0:T(8,128)(2,1)} %param.9, f32[1536]{0:T(1024)} %param.10), kind=kOutput, calls=%fused_computation.3 | convolution fusion | flops 2416705536 | bytes 9443328 | tf_op jit(solution)/shard_map/dot_general | solution.py:20
  43.0 0.0 copy-start.3
  43.0 1.7 copy-done.3
  44.6 0.0 copy-done.2
  44.6 6.4 %convolution_convert_fusion = bf16[512,1536]{1,0:T(8,128)(2,1)} fusion(bf16[1536,1536]{1,0:T(8,128)(2,1)} %param.9, f32[1536]{0:T(1024)S(1)} %copy-done.2, f32[512,1536]{1,0:T(8,128)S(1)} %convolution_add_fusion.1), kind=kOutput, calls=%fused_computation.11 | convolution fusion | flops 2423783424 | bytes 9443328 | tf_op jit(solution)/shard_map/dot_general | solution.py:27
  51.1 0.0 reduce-scatter.3.cloned.1.call-update
  51.1 0.0 all-gather.5.cloned.1.call-start
  51.1 33.9 %reduce-scatter.3.cloned.1.call-done = bf16[64,1536]{1,0:T(8,128)(2,1)} async-done(((bf16[512,1536]{1,0:T(8,128)(2,1)}), bf16[64,1536]{1,0:T(8,128)(2,1)}) %reduce-scatter.3.cloned.1.call-update) | async-done | bytes 196624 | tf_op jit(solution)/shard_map/reduce_scatter | solution.py:26
  85.0 1.1 fusion.8
  86.1 0.6 multiply_reduce_fusion.1
  86.7 1.7 fusion.9
  88.4 0.0 all-gather.5.cloned.1.call-update
  88.4 0.0 copy-start
  88.4 0.0 reduce-scatter.5.cloned.1.call-start
  88.5 23.0 %all-gather.5.cloned.1.call-done = bf16[512,1536]{1,0:T(8,128)(2,1)} async-done(((bf16[64,1536]{1,0:T(8,128)(2,1)}), bf16[512,1536]{1,0:T(8,128)(2,1)}) %all-gather.5.cloned.1.call-update) | async-done | bytes 1572880 | tf_op jit(solution)/shard_map/all_gather | solution.py:38
  111.5 7.8 %fusion.12 = (f32[1536]{0:T(1024)S(1)}, bf16[512,1536]{1,0:T(8,128)(2,1)S(1)}, f32[1536]{0:T(1024)S(1)}) fusion(f32[512,1536]{1,0:T(8,128)} %copy-done.3, f32[1536]{0:T(1024)S(1)} %copy-done.2, bf16[512,1536]{1,0:T(8,128)(2,1)} %all-gather.5.cloned.1.call-done, bf16[1536,1536]{1,0:T(8,128)(2,1)} %param.9), kind=kOutput, calls=%fused_computation.26 | convolution fusion | flops 2430858240 | bytes 11028480 | tf_op jit(solution)/shard_map/dot_general | solution.py:40
  119.4 0.0 copy-done
  119.4 0.0 copy-start.1
  119.4 0.0 copy-start.4
  119.4 2.7 %fusion.4 = f32[1536,1536]{1,0:T(8,128)S(1)} fusion(bf16[512,1536]{1,0:T(8,128)(2,1)S(1)} %copy-done, bf16[512,1536]{1,0:T(8,128)(2,1)S(1)} %get-tuple-element.7), kind=kOutput, calls=%fused_computation.12 | convolution fusion | flops 2415919104 | bytes 12582912 | tf_op jit(solution)/shard_map/dot_general | solution.py:8
  122.1 5.8 %convolution_add_fusion = f32[1536,1536]{1,0:T(8,128)} fusion(f32[1536,1536]{1,0:T(8,128)S(1)} %fusion.4, bf16[512,1536]{1,0:T(8,128)(2,1)S(1)} %copy-done.1, f32[1536]{0:T(1024)S(1)} %copy-done.2, f32[512,1536]{1,0:T(8,128)S(1)} %copy-done.4), kind=kOutput, calls=%fused_computation | convolution fusion | flops 2425356288 | bytes 23599104 | tf_op jit(solution)/shard_map/dot_general | solution.py:8
  127.9 0.0 reduce-scatter.5.cloned.1.call-update
  127.9 40.7 %psum.23 = f32[]{:T(128)} all-reduce(f32[]{:T(128)} %get-tuple-element.9), channel_id=1, replica_groups=mesh['dp'=4,'tensor'=8] {'dp','tensor'}, use_global_device_ids=true, to_apply=%region_8.0 | all-reduce | flops 1 | bytes 8 | tf_op jit(solution)/shard_map/psum | solution.py:37
  169.3 17.3 %all-reduce = (f32[1536]{0:T(1024)}, f32[1536]{0:T(1024)}) all-reduce(f32[1536]{0:T(1024)S(1)} %get-tuple-element.6, f32[1536]{0:T(1024)S(1)} %get-tuple-element.8), channel_id=1, replica_groups=mesh['dp'=4,'tensor'=8] {'dp'}, use_global_device_ids=true, to_apply=%region_4.0 | all-reduce | flops 3072 | bytes 24576 | tf_op jit(solution)/shard_map/psum | solution.py:46
  186.6 37.5 %reduce-scatter.5.cloned.1.call-done = f32[384,1536]{1,0:T(8,128)} async-done(((f32[1536,1536]{1,0:T(8,128)}), f32[384,1536]{1,0:T(8,128)}) %reduce-scatter.5.cloned.1.call-update) | async-done | bytes 2359312 | tf_op jit(solution)/shard_map/reduce_scatter | solution.py:45
  (2 shorter events, 0.0 us)
Async XLA Ops:
  7.2 30.8 %all-gather.3.cloned.1.call-start = ((), (), s32[]{:S(2)}) async-start(), calls=%async_computation.2 | async-start | bytes 1769472 | tf_op jit(solution)/shard_map/all_gather | solution.py:19
  9.7 34.9 %copy-start.2 = (f32[1536]{0:T(1024)S(1)}, f32[1536]{0:T(1024)}, u32[]{:S(2)}) copy-start(f32[1536]{0:T(1024)} %param.11) | copy-start | bytes 18436
  9.7 75.3 %reduce-scatter.3.cloned.1.call-start = ((), (), s32[]{:S(2)}) async-start(), calls=%async_computation.3 | async-start | bytes 1769472 | tf_op jit(solution)/shard_map/reduce_scatter | solution.py:26
  43.0 1.7 copy-start.3
  51.1 60.4 %all-gather.5.cloned.1.call-start = ((), (), s32[]{:S(2)}) async-start(), calls=%async_computation.4 | async-start | bytes 1769472 | tf_op jit(solution)/shard_map/all_gather | solution.py:38
  88.4 31.0 %copy-start = (bf16[512,1536]{1,0:T(8,128)(2,1)S(1)}, bf16[512,1536]{1,0:T(8,128)(2,1)}, u32[]{:S(2)}) copy-start(bf16[512,1536]{1,0:T(8,128)(2,1)} %all-gather.3.cloned.1.call-done) | copy-start | bytes 4718596
  88.4 135.6 %reduce-scatter.5.cloned.1.call-start = ((), (), s32[]{:S(2)}) async-start(), calls=%async_computation.5 | async-start | bytes 11796480 | tf_op jit(solution)/shard_map/reduce_scatter | solution.py:45
  119.4 2.7 %copy-start.1 = (bf16[512,1536]{1,0:T(8,128)(2,1)S(1)}, bf16[512,1536]{1,0:T(8,128)(2,1)}, u32[]{:S(2)}) copy-start(bf16[512,1536]{1,0:T(8,128)(2,1)} %all-gather.5.cloned.1.call-done) | copy-start | bytes 4718596
  119.4 2.7 %copy-start.4 = (f32[512,1536]{1,0:T(8,128)S(1)}, f32[512,1536]{1,0:T(8,128)}, u32[]{:S(2)}) copy-start(f32[512,1536]{1,0:T(8,128)} %copy-done.3) | copy-start | bytes 9437188
Sparse Core Ops, SparseCore 0:
  10.2 27.7 all-gather.2
  51.2 33.7 reduce-scatter.2
  88.5 22.9 all-gather.4
  128.0 96.0 reduce-scatter.4
where the time goes:
time: 232 us
  waiting for transfers between devices  123 us (53%)
  blocking collectives  58.1 us (25%)
  matrix products  27.6 us (12%)
  between operations  15.6 us (7%)
  other arithmetic  5.86 us (3%)
    psum x1, blocking collectives, local(): loss = lax.psum(jnp.sum((norm - 1.0) ** 2), ('dp', 'tensor'))  40.7 us
    reduce_scatter x1, waiting for transfers between devices, local(): grad_w = lax.psum_scatter(partial_w, 'dp', scatter_dimension=0, tiled=True)  37.5 us
    reduce_scatter x1, waiting for transfers between devices, local(): lax.psum_scatter(lax.dot_general(u, w_first, (((1,), (1,)), ((), ())), pr...  33.9 us
    all_gather x1, waiting for transfers between devices, local(): group = lax.all_gather(mixed, 'tensor', axis=0, tiled=True)  28.2 us
    all_gather x1, waiting for transfers between devices, local(): big = lax.all_gather(scaled, 'tensor', axis=0, tiled=True)  23 us
    psum x1, blocking collectives, local(): lax.psum((jnp.sum(dz, axis=0), jnp.sum(p * d1, axis=0)), 'dp')  17.3 us
    dot_general x2, matrix products, row_contract(): lax.dot_general(left, right, (((0,), (0,)), ((), ())), preferred_element_...  8.42 us
    dot_general x1, matrix products, local(): p = jnp.dot(big, w_first, preferred_element_type=jnp.float32)  7.84 us
  transfers between devices with their start and end apart: 4, of which 4 were waited for; matrix products, arithmetic and copies ran while one was open for 0% of the time, Pallas kernels for 0%

commit v1 on v0

--- a/solution.py
+++ b/solution.py
@@ -1,7 +1,15 @@
+import functools
+
 import jax
 import jax.numpy as jnp
 from jax import lax
+from jax.experimental import pallas as pl
+from jax.experimental.pallas import tpu as pltpu
 from jax.sharding import PartitionSpec as P
+
+MESH = pl.DeviceIdType.MESH
+VMEM_BYTES = 62 * 2**20
+HELD_BYTES = 58 * 2**20
 
 
 def row_contract(left, right):
@@ -47,6 +55,326 @@
     return (grad_w, grad_bias, grad_head, penalty)
 
 
+def flip(index, mask):
+    bit = 1
+    while bit <= mask:
+        if mask & bit:
+            index = index + bit - 2 * bit * lax.rem(index // bit, 2)
+        bit *= 2
+    return index
+
+
+class Gather:
+    def __init__(self, held, nz, send, recv, dev):
+        self.held, self.nz, self.dev = held, nz, dev
+        self.send, self.recv = send, recv
+        self.names = (
+            [("z", 0, k) for k in range(1, nz)]
+            + [(kind, dx, k) for kind, dxs in (("c", range(4)), ("xy", (1, 2)), ("d", (0, 1)))
+               for dx in dxs for k in range(nz)]
+        )
+
+    def copy(self, name):
+        kind, dx, k = name
+        held, dev = self.held, self.dev
+        half = held.shape[3] // 2
+        if kind == "z":
+            src, dst, to = held.at[0, 0, 0], held.at[0, k, 0], dev(0, k, 0)
+        elif kind == "c":
+            src, dst, to = held.at[dx, k, 0], held.at[dx, k, 1], dev(0, 0, 1)
+        elif kind == "xy":
+            src, dst, to = held.at[0, k, 0], held.at[dx, k, 0], dev(dx, 0, 0)
+        else:
+            rows = pl.ds(dx * half, half)
+            src, dst, to = held.at[1 + dx, k, 0, rows], held.at[3, k, 0, rows], dev(2 - dx, 0, 0)
+        i = self.names.index(name)
+        return pltpu.make_async_remote_copy(
+            src_ref=src, dst_ref=dst, send_sem=self.send.at[i], recv_sem=self.recv.at[i],
+            device_id=to, device_id_type=MESH,
+        )
+
+    def start(self):
+        for k in range(1, self.nz):
+            self.copy(("z", 0, k)).start()
+        self.spread(0)
+
+    def spread(self, k):
+        if k:
+            self.copy(("z", 0, k)).wait_recv()
+        for name in (("xy", 1, k), ("xy", 2, k), ("c", 0, k)):
+            self.copy(name).start()
+
+    def turn(self, k):
+        for dx in (1, 2):
+            self.copy(("xy", dx, k)).wait_recv()
+            self.copy(("d", dx - 1, k)).start()
+            self.copy(("c", dx, k)).start()
+
+    def last(self, k):
+        self.copy(("d", 0, k)).wait_recv()
+        self.copy(("d", 1, k)).wait_recv()
+        self.copy(("c", 3, k)).start()
+
+    def arrived(self, dx, ks):
+        for k in ks:
+            self.copy(("c", dx, k)).wait_recv()
+
+    def finish(self):
+        for name in self.names:
+            self.copy(name).wait_send()
+
+
+def kernel(
+    nz, tile, total_rows,
+    real, fake, mix, w_hbm, bias, head,
+    out, out_bias, out_head, out_pen,
+    w, mixed, big, u, d1, d2, own, lhs, to_pair, from_pair, to_z, from_z,
+    sum_bias, sum_head, loss, loss_in,
+    w_sem, m_send, m_recv, b_send, b_recv, p_send, p_recv, z_send, z_recv, l_send, l_recv,
+):
+    f32, bf16 = jnp.float32, jnp.bfloat16
+    dp, tensor = lax.axis_index("dp"), lax.axis_index("tensor")
+    z_at, core = tensor // 2, lax.rem(tensor, 2)
+    rows, feats = real.shape
+    hidden = w.shape[1]
+    part = out.shape[0]
+    pairs = nz // 2
+
+    def dev(dx, zx, cc):
+        return (flip(dp, dx), flip(z_at, zx) * 2 + flip(core, cc))
+
+    load_w = pltpu.make_async_copy(w_hbm, w, w_sem)
+    load_w.start()
+    partners = [dev(0, 0, 1), dev(1, 0, 0), dev(2, 0, 0)]
+    partners += [dev(0, k, 0) for k in range(1, nz)]
+    barrier = pltpu.get_barrier_semaphore()
+    for to in partners:
+        pl.semaphore_signal(barrier, inc=1, device_id=to, device_id_type=MESH)
+    coef = mix[...].astype(f32) / 256.0
+    real_f = real[...].astype(f32)
+    mixed[0, 0, 0] = (real_f + coef * (fake[...].astype(f32) - real_f)).astype(bf16)
+    pl.semaphore_wait(barrier, len(partners))
+
+    m_all = Gather(mixed, nz, m_send, m_recv, dev)
+    b_all = Gather(big, nz, b_send, b_recv, dev)
+
+    def block(held, dx, h):
+        return held[dx, 2 * h:2 * h + 2].reshape(4 * rows, feats)
+
+    def columns(i):
+        return pl.ds(pl.multiple_of(i * tile, tile), tile)
+
+    def hidden_units(dx, h):
+        m_all.arrived(dx, (2 * h, 2 * h + 1))
+
+        def step(i, carry):
+            cols = columns(i)
+            z = jnp.dot(block(mixed, dx, h), w[:, cols], preferred_element_type=f32)
+            z = z + bias[:, cols]
+            t = jnp.tanh(0.5 * z)
+            sg = 0.5 + 0.5 * t
+            slope = 0.25 * (1.0 - t * t)
+            first = sg + z * slope
+            second = slope * (2.0 - z * t)
+            head_row = head[:, cols]
+            d1[dx, h, :, cols] = first
+            d2[dx, h, :, cols] = second * head_row
+            u[dx, h, :, cols] = (first * head_row).astype(bf16)
+            return carry
+
+        lax.fori_loop(0, hidden // tile, step, 0)
+
+    def pair_copy(k):
+        return pltpu.make_async_remote_copy(
+            src_ref=to_pair.at[k], dst_ref=from_pair.at[k], send_sem=p_send.at[k],
+            recv_sem=p_recv.at[k], device_id=dev(0, 0, 1), device_id_type=MESH,
+        )
+
+    def z_copy(k):
+        return pltpu.make_async_remote_copy(
+            src_ref=to_z.at[k], dst_ref=from_z.at[k], send_sem=z_send.at[k],
+            recv_sem=z_recv.at[k], device_id=dev(0, k, 0), device_id_type=MESH,
+        )
+
+    def input_gradient(h):
+        def step(i, carry):
+            cols = columns(i)
+            g = lax.dot_general(
+                u[0, h], w[cols, :], (((1,), (1,)), ((), ())), preferred_element_type=f32
+            ).reshape(2, 2, rows, tile)
+            for j in range(2):
+                own[2 * h + j, :, cols] = g[j, 0]
+                to_pair[2 * h + j, :, cols] = g[j, 1].astype(bf16)
+            return carry
+
+        lax.fori_loop(0, feats // tile, step, 0)
+        for j in range(2):
+            pair_copy(2 * h + j).start()
+
+    def pair_sum(k):
+        pair_copy(k).wait_recv()
+        both = own[k] + from_pair[k].astype(f32)
+        if k:
+            to_z[k] = both.astype(bf16)
+            z_copy(k).start()
+        else:
+            own[0] = both
+
+    def weight_terms(dx, h, start):
+        b_all.arrived(dx, (2 * h, 2 * h + 1))
+        mine = pl.ds(pl.multiple_of(dp * part, 128), part)
+        for j, held in enumerate((mixed, big)):
+            lhs[j] = held[dx, 2 * h:2 * h + 2, :, :, mine].reshape(4 * rows, part).T
+
+        def step(i, carry):
+            cols = columns(i)
+            p = jnp.dot(block(big, dx, h), w[:, cols], preferred_element_type=f32)
+            dz = p * d2[dx, h, :, cols]
+            ph = p * d1[dx, h, :, cols]
+            add_bias = jnp.sum(dz.reshape(4 * rows // 8, 8, tile), axis=0)
+            add_head = jnp.sum(ph.reshape(4 * rows // 8, 8, tile), axis=0)
+            if h == 0:
+                sum_bias[dx, :, cols] = add_bias
+                sum_head[dx, :, cols] = add_head
+            else:
+                sum_bias[dx, :, cols] += add_bias
+                sum_head[dx, :, cols] += add_head
+            term = jnp.dot(lhs[0], dz.astype(bf16), preferred_element_type=f32)
+            term = term + jnp.dot(lhs[1], u[dx, h, :, cols], preferred_element_type=f32)
+            if start:
+                out[:, cols] = term
+            else:
+                out[:, cols] += term
+            return carry
+
+        lax.fori_loop(0, hidden // tile, step, 0)
+
+    def loss_copy(i, to):
+        return pltpu.make_async_remote_copy(
+            src_ref=loss.at[i], dst_ref=loss_in.at[i], send_sem=l_send.at[i],
+            recv_sem=l_recv.at[i], device_id=to, device_id_type=MESH,
+        )
+
+    m_all.start()
+    load_w.wait()
+    for h in range(pairs):
+        for k in (2 * h, 2 * h + 1):
+            if k:
+                m_all.spread(k)
+        hidden_units(0, h)
+        input_gradient(h)
+        if h:
+            for k in (2 * h - 2, 2 * h - 1):
+                pair_sum(k)
+    for k in (nz - 2, nz - 1):
+        pair_sum(k)
+
+    for h in range(pairs):
+        for k in (2 * h, 2 * h + 1):
+            m_all.turn(k)
+        hidden_units(1, h)
+    for h in range(pairs):
+        hidden_units(2, h)
+
+    g = own[0]
+    for k in range(1, nz):
+        z_copy(k).wait_recv()
+        g = g + from_z[k].astype(f32)
+    norm = jnp.sqrt(jnp.sum(g * g, axis=1, keepdims=True) + 1e-06)
+    big[0, 0, 0] = (20.0 * (norm - 1.0) / norm * g).astype(bf16)
+    b_all.start()
+    miss = jnp.sum((norm - 1.0) ** 2, axis=0, keepdims=True)
+    loss[0] = jnp.broadcast_to(miss, loss.shape[1:])
+
+    hops = [dev(0, 0, 1)]
+    bit = 1
+    while bit < nz:
+        hops.append(dev(0, bit, 0))
+        bit *= 2
+    hops += [dev(1, 0, 0), dev(2, 0, 0)]
+    loss_copy(0, hops[0]).start()
+    state = [0]
+
+    def loss_step():
+        i = state[0]
+        if i < len(hops):
+            loss_copy(i, hops[i]).wait_recv()
+            loss[i + 1] = loss[i] + loss_in[i]
+            if i + 1 < len(hops):
+                loss_copy(i + 1, hops[i + 1]).start()
+            state[0] = i + 1
+
+    for k in range(nz):
+        m_all.last(k)
+    for h in range(pairs):
+        for k in (2 * h, 2 * h + 1):
+            if k:
+                b_all.spread(k)
+        hidden_units(3, h)
+        loss_step()
+
+    order = []
+    for h in range(pairs):
+        order.append((0, h))
+    for h in range(pairs):
+        order.append((1, h))
+        order.append((2, h))
+    for h in range(pairs):
+        order.append((3, h))
+    turned, ended = 0, 0
+    for n, (dx, h) in enumerate(order):
+        while turned < nz and (turned <= n or (dx and turned < 2 * h + 2)):
+            b_all.turn(turned)
+            turned += 1
+        while ended < nz and (dx == 3 and ended < 2 * h + 2 or ended + nz <= n):
+            b_all.last(ended)
+            ended += 1
+        weight_terms(dx, h, n == 0)
+        loss_step()
+    while state[0] < len(hops):
+        loss_step()
+
+    for ref, sums in ((out_bias, sum_bias), (out_head, sum_head)):
+        whole = (sums[0] + sums[1]) + (sums[2] + sums[3])
+        ref[...] = jnp.sum(whole, axis=0, keepdims=True)
+    out_pen[...] = 10.0 * loss[len(hops)] / total_rows
+
+    m_all.finish()
+    b_all.finish()
+    for k in range(nz):
+        pair_copy(k).wait_send()
+        if k:
+            z_copy(k).wait_send()
+    for i, to in enumerate(hops):
+        loss_copy(i, to).wait_send()
+
+
+def scratch_of(rows, feats, hidden, part, nz):
+    f32, bf16 = jnp.float32, jnp.bfloat16
+    hops = nz.bit_length() + 2
+    held = [
+        ((feats, hidden), bf16),
+        ((4, nz, 2, rows, feats), bf16),
+        ((4, nz, 2, rows, feats), bf16),
+        ((4, nz // 2, 4 * rows, hidden), bf16),
+        ((4, nz // 2, 4 * rows, hidden), f32),
+        ((4, nz // 2, 4 * rows, hidden), f32),
+        ((nz, rows, feats), f32),
+        ((2, part, 4 * rows), bf16),
+        ((nz, rows, feats), bf16),
+        ((nz, rows, feats), bf16),
+        ((nz, rows, feats), bf16),
+        ((nz, rows, feats), bf16),
+        ((4, 8, hidden), f32),
+        ((4, 8, hidden), f32),
+        ((hops + 1, 8, 128), f32),
+        ((hops + 1, 8, 128), f32),
+    ]
+    moves = nz - 1 + 8 * nz
+    sems = [(), (moves,), (moves,), (moves,), (moves,), (nz,), (nz,), (nz,), (nz,), (hops,), (hops,)]
+    return held, sems
+
+
 def solution(mesh):
     placed = (
         P(("dp", "tensor"), None),
@@ -56,8 +384,46 @@
         P("tensor"),
         P("tensor"),
     )
+    groups, members = mesh.shape["dp"], mesh.shape["tensor"]
+    nz = members // 2
+
+    def body(real_feats, fake_feats, mix_num, w_first, bias, head):
+        rows, feats = real_feats.shape
+        hidden = w_first.shape[1]
+        part = feats // groups
+        held, sems = scratch_of(rows, feats, hidden, part, max(nz, 2))
+        size = part * hidden * 4
+        for shape, dtype in held:
+            size += functools.reduce(lambda a, b: a * b, shape) * jnp.dtype(dtype).itemsize
+        tile = next((t for t in (512, 256, 128) if hidden % t == 0 and feats % t == 0), 0)
+        fits = (
+            groups == 4 and members % 2 == 0 and nz >= 2 and nz & (nz - 1) == 0
+            and tile and rows % 32 == 0 and part % 128 == 0 and size <= HELD_BYTES
+        )
+        if not fits:
+            return local(real_feats, fake_feats, mix_num, w_first, bias, head)
+        vmem = pl.BlockSpec(memory_space=pltpu.VMEM)
+        total_rows = rows * groups * members
+        grad_w, grad_bias, grad_head, pen = pl.pallas_call(
+            functools.partial(kernel, nz, tile, total_rows),
+            out_shape=(
+                jax.ShapeDtypeStruct((part, hidden), jnp.float32),
+                jax.ShapeDtypeStruct((1, hidden), jnp.float32),
+                jax.ShapeDtypeStruct((1, hidden), jnp.float32),
+                jax.ShapeDtypeStruct((8, 128), jnp.float32),
+            ),
+            in_specs=[vmem, vmem, vmem, pl.BlockSpec(memory_space=pl.ANY), vmem, vmem],
+            out_specs=(vmem, vmem, vmem, vmem),
+            scratch_shapes=[pltpu.VMEM(s, t) for s, t in held]
+            + [pltpu.SemaphoreType.DMA(s) if s else pltpu.SemaphoreType.DMA for s in sems],
+            compiler_params=pltpu.CompilerParams(
+                collective_id=0, has_side_effects=True, vmem_limit_bytes=VMEM_BYTES
+            ),
+        )(real_feats, fake_feats, mix_num[:, None], w_first, bias[None], head[None])
+        return (grad_w, grad_bias[0], grad_head[0], pen[0, 0])
+
     return jax.shard_map(
-        local,
+        body,
         mesh=mesh,
         in_specs=placed,
         out_specs=(P("dp", "tensor"), P("tensor"), P("tensor"), P()),

time: 232 us -> 111 us (0.48)
  waiting for transfers between devices: 123 us -> 0 us
  Pallas kernels: 0 us -> 98.2 us
  blocking collectives: 58.1 us -> 0 us
  matrix products: 27.6 us -> 0 us
  between operations: 15.6 us -> 0.64 us
  local copies, waits for them, and re-layouts: 1.68 us -> 8.36 us
  other arithmetic: 5.86 us -> 2.62 us
    pallas_call x0 -> x1, Pallas kernels: none -> 98.2 us  [body(): pl.pallas_call(functools.partial(kernel, nz, tile, total_rows), out_shape...]
    reduce_scatter x2 -> x0, waiting for transfers between devices: 71.3 us -> none  [the longest x1 37.5 us: local(): grad_w = lax.psum_scatter(partial_w, 'dp', scatter_dimension=0, tiled=True)]
    psum x2 -> x0, blocking collectives: 58.1 us -> none  [the longest x1 40.7 us: local(): loss = lax.psum(jnp.sum((norm - 1.0) ** 2), ('dp', 'tensor'))]
    all_gather x2 -> x0, waiting for transfers between devices: 51.3 us -> none  [the longest x1 28.2 us: local(): group = lax.all_gather(mixed, 'tensor', axis=0, tiled=True)]
    dot_general x5 -> x0, matrix products: 27.6 us -> none  [the longest x2 8.42 us: row_contract(): lax.dot_general(left, right, (((0,), (0,)), ((), ())), preferred_element_...]
    broadcast_in_dim x0 -> x3, local copies, waits for them, and re-layouts: none -> 3.95 us  [the longest x1 1.36 us: body(): mix_num[:, None]]
    convert_element_type x2 -> x0, other arithmetic: 3.52 us -> none  [the longest x1 1.81 us: local(): (real_f + coef[:, None] * (fake_feats.astype(jnp.float32) - real_f)).asty...]
    pallas_call x0 -> x2, other arithmetic: none -> 2.62 us  [body(): pl.pallas_call(functools.partial(kernel, nz, tile, total_rows), out_shape...]
  transfers between devices with their start and end apart: 4 -> 0, of which waited for: 4 -> 0; matrix products, arithmetic and copies ran while one was open for 0% -> 0% of each run, Pallas kernels for 0% -> 0%
where the time goes in v1:
time: 111 us; the launch traced here: 110 us
  Pallas kernels  98.2 us (88%)
  local copies, waits for them, and re-layouts  8.36 us (8%)
  other arithmetic  2.62 us (2%)
    pallas_call x1, Pallas kernels, body(): pl.pallas_call(functools.partial(kernel, nz, tile, total_rows), out_shape...  98.2 us
    unnamed x1, local copies, waits for them, and re-layouts  3.22 us
    pallas_call x2, other arithmetic, body(): pl.pallas_call(functools.partial(kernel, nz, tile, total_rows), out_shape...  2.62 us

profile of v1, /device:TPU:0, one launch (start us, length us, event | category | flops | bytes accessed | tf_op | source)
XLA Modules:
  0.0 109.8 jit_solution(14789000398897987207)
XLA Ops:
  0.6 1.3 %broadcast_in_dim.10.bias = f32[1,1536]{1,0:T(1,128)} reshape(f32[1536]{0:T(1024)} %param.10) | data formatting | bytes 12288 | tf_op jit(solution)/shard_map/broadcast_in_dim | solution.py:422
  1.9 1.3 %broadcast_in_dim.11.head = f32[1,1536]{1,0:T(1,128)} reshape(f32[1536]{0:T(1024)} %param.11) | data formatting | bytes 12288 | tf_op jit(solution)/shard_map/broadcast_in_dim | solution.py:422
  3.2 1.4 %copy.10.mix = s32[64,1]{1,0:T(8,128)} copy(s32[64,1]{0,1:T(1,128)} %bitcast.2) | data formatting | bytes 512 | tf_op jit(solution)/shard_map/broadcast_in_dim | solution.py:422
  4.6 98.2 %shard_map.93 = (f32[384,1536]{1,0:T(8,128)}, f32[1,1536]{1,0:T(1,128)}, f32[1,1536]{1,0:T(1,128)}, f32[8,128]{1,0:T(8,128)}) custom-call(bf16[64,1536]{1,0:T(8,128)(2,1)} %real.1, bf16[64,1536]{1,0:T(8,128)(2,1)} %fake.1, s32[64,1]{1,0:T(8,128)} %copy.10.mix, bf16[1536,1536]{1,0:T(8,128)(2,1)} %w_hbm.1, f32[1,1536]{1,0:T(1,128)} %broadcast_in_dim.10.bias, ...), custom_call_target="tpu_custom_call" | custom-call | tf_op jit(solution)/shard_map/pallas_call | solution.py:407
  102.8 1.2 %slice.3 = f32[1,1]{1,0:T(1,128)} slice(f32[8,128]{1,0:T(8,128)} %get-tuple-element.11), slice={[0:1], [0:1]} | slice | bytes 8 | tf_op jit(solution)/shard_map/slice | solution.py:423
  104.0 1.3 %reduce = f32[1536]{0:T(1024)} reduce(f32[1,1536]{1,0:T(1,128)} %get-tuple-element.9, f32[]{:T(128)} %constant), dimensions={0}, to_apply=%get-tuple-element.9.reduce_sub_computation | reduce | bytes 12292 | tf_op jit(solution)/shard_map/pallas_call | solution.py:407
  105.3 1.3 %reduce.1 = f32[1536]{0:T(1024)} reduce(f32[1,1536]{1,0:T(1,128)} %get-tuple-element.10, f32[]{:T(128)} %constant), dimensions={0}, to_apply=%get-tuple-element.10.reduce_sub_computation | reduce | bytes 12292 | tf_op jit(solution)/shard_map/pallas_call | solution.py:407
  106.6 3.2 %copy.12 = f32[384,1536]{1,0:T(8,128)} copy(f32[384,1536]{1,0:T(8,128)} %get-tuple-element.16) | data formatting | bytes 4718592

commit v2 on v1

v2 whole, which is shorter than its diff:
```python
import functools

import jax
import jax.numpy as jnp
from jax import lax
from jax.experimental import pallas as pl
from jax.experimental.pallas import tpu as pltpu
from jax.sharding import PartitionSpec as P

MESH = pl.DeviceIdType.MESH
VMEM_BYTES = 62 * 2**20
HELD_BYTES = 58 * 2**20


def row_contract(left, right):
    return lax.dot_general(
        left, right, (((0,), (0,)), ((), ())), preferred_element_type=jnp.float32
    )


def local(real_feats, fake_feats, mix_num, w_first, bias, head):
    coef = mix_num.astype(jnp.float32) / 256.0
    real_f = real_feats.astype(jnp.float32)
    mixed = (real_f + coef[:, None] * (fake_feats.astype(jnp.float32) - real_f)).astype(
        jnp.bfloat16
    )
    group = lax.all_gather(mixed, "tensor", axis=0, tiled=True)
    z = jnp.dot(group, w_first, preferred_element_type=jnp.float32) + bias
    sg = jax.nn.sigmoid(z)
    d1 = sg * (1.0 + z * (1.0 - sg))
    d2 = sg * (1.0 - sg) * (2.0 + z * (1.0 - 2.0 * sg))
    u = (d1 * head).astype(jnp.bfloat16)
    total_rows = group.shape[0] * lax.axis_size("dp")
    grad_in = lax.psum_scatter(
        lax.dot_general(
            u, w_first, (((1,), (1,)), ((), ())), preferred_element_type=jnp.float32
        ).astype(jnp.bfloat16),
        "tensor",
        scatter_dimension=0,
        tiled=True,
    ).astype(jnp.float32)
    norm = jnp.sqrt(jnp.sum(grad_in * grad_in, axis=1) + 1e-06)
    scale = 20.0 * (norm - 1.0) / norm
    scaled = (scale[:, None] * grad_in).astype(jnp.bfloat16)
    loss = lax.psum(jnp.sum((norm - 1.0) ** 2), ("dp", "tensor"))
    big = lax.all_gather(scaled, "tensor", axis=0, tiled=True)
    penalty = 10.0 * loss / total_rows
    p = jnp.dot(big, w_first, preferred_element_type=jnp.float32)
    dz = p * head * d2
    dzb = dz.astype(jnp.bfloat16)
    partial_w = row_contract(group, dzb)
    partial_w = partial_w + row_contract(big, u)
    grad_w = lax.psum_scatter(partial_w, "dp", scatter_dimension=0, tiled=True)
    grad_bias, grad_head = lax.psum((jnp.sum(dz, axis=0), jnp.sum(p * d1, axis=0)), "dp")
    return (grad_w, grad_bias, grad_head, penalty)


def flip(index, mask):
    bit = 1
    while bit <= mask:
        if mask & bit:
            index = index + bit - 2 * bit * lax.rem(index // bit, 2)
        bit *= 2
    return index


class Gather:
    def __init__(self, held, nz, send, recv, dev):
        self.held, self.nz, self.dev = held, nz, dev
        self.send, self.recv = send, recv
        self.names = (
            [("z", 0, k) for k in range(1, nz)]
            + [(kind, dx, k) for kind, dxs in (("c", range(4)), ("xy", (1, 2)), ("d", (0, 1)))
               for dx in dxs for k in range(nz)]
        )

    def copy(self, name):
        kind, dx, k = name
        held, dev = self.held, self.dev
        half = held.shape[3] // 2
        if kind == "z":
            src, dst, to = held.at[0, 0, 0], held.at[0, k, 0], dev(0, k, 0)
        elif kind == "c":
            src, dst, to = held.at[dx, k, 0], held.at[dx, k, 1], dev(0, 0, 1)
        elif kind == "xy":
            src, dst, to = held.at[0, k, 0], held.at[dx, k, 0], dev(dx, 0, 0)
        else:
            rows = pl.ds(dx * half, half)
            src, dst, to = held.at[1 + dx, k, 0, rows], held.at[3, k, 0, rows], dev(2 - dx, 0, 0)
        i = self.names.index(name)
        return pltpu.make_async_remote_copy(
            src_ref=src, dst_ref=dst, send_sem=self.send.at[i], recv_sem=self.recv.at[i],
            device_id=to, device_id_type=MESH,
        )

    def start(self):
        for k in range(1, self.nz):
            self.copy(("z", 0, k)).start()
        self.spread(0)

    def spread(self, *ks):
        for k in ks:
            if k:
                self.copy(("z", 0, k)).wait_recv()
            for name in (("xy", 1, k), ("xy", 2, k), ("c", 0, k)):
                self.copy(name).start()

    def turn(self, *ks):
        for k in ks:
            for dx in (1, 2):
                self.copy(("xy", dx, k)).wait_recv()
                self.copy(("d", dx - 1, k)).start()
                self.copy(("c", dx, k)).start()

    def last(self, *ks):
        for k in ks:
            self.copy(("d", 0, k)).wait_recv()
            self.copy(("d", 1, k)).wait_recv()
            self.copy(("c", 3, k)).start()

    def arrived(self, dx):
        for k in range(self.nz):
            self.copy(("c", dx, k)).wait_recv()

    def finish(self):
        for name in self.names:
            self.copy(name).wait_send()


def kernel(
    nz, tile, total_rows,
    real, fake, mix, w_hbm, bias, head,
    out, out_bias, out_head, out_pen,
    w, mixed, big, u, d1, d2, own, lhs, to_pair, from_pair, to_z, from_z,
    sum_bias, sum_head, loss, loss_in, bias_row, head_row,
    w_sem, m_send, m_recv, b_send, b_recv, p_send, p_recv, z_send, z_recv, l_send, l_recv,
):
    f32, bf16 = jnp.float32, jnp.bfloat16
    dp, tensor = lax.axis_index("dp"), lax.axis_index("tensor")
    z_at, core = tensor // 2, lax.rem(tensor, 2)
    feats = real.shape[1]
    rows = real.shape[0] // 2
    lot = 2 * nz * rows
    hidden = w.shape[1]
    part = out.shape[0]
    every, others = tuple(range(nz)), tuple(range(1, nz))

    def dev(dx, zx, cc):
        return (flip(dp, dx), flip(z_at, zx) * 2 + flip(core, cc))

    load_w = pltpu.make_async_copy(w_hbm, w, w_sem)
    load_w.start()
    partners = [dev(0, 0, 1), dev(1, 0, 0), dev(2, 0, 0)]
    partners += [dev(0, k, 0) for k in others]
    barrier = pltpu.get_barrier_semaphore()
    for to in partners:
        pl.semaphore_signal(barrier, inc=1, device_id=to, device_id_type=MESH)
    count = mix.shape[0]
    places = [lax.broadcasted_iota(jnp.int32, (count, count), axis) for axis in (0, 1)]
    spread = jnp.broadcast_to(mix[...].reshape(1, count).astype(f32), (count, count))
    spread = jnp.where(places[0] == places[1], spread, 0.0)
    coef = jnp.sum(spread, axis=1, keepdims=True) / 256.0
    real_f = real[...].astype(f32)
    rows_in = (real_f + coef * (fake[...].astype(f32) - real_f)).astype(bf16)
    for h in range(2):
        mixed[h, 0, 0, 0] = rows_in[h * rows:(h + 1) * rows]
    bias_row[...] = bias[...].reshape(1, hidden)
    head_row[...] = head[...].reshape(1, hidden)
    pl.semaphore_wait(barrier, len(partners))

    m_all = [Gather(mixed.at[h], nz, m_send.at[h], m_recv.at[h], dev) for h in range(2)]
    b_all = [Gather(big.at[h], nz, b_send.at[h], b_recv.at[h], dev) for h in range(2)]

    def block(held, dx, h):
        return held[h, dx].reshape(lot, feats)

    def columns(i):
        return pl.ds(pl.multiple_of(i * tile, tile), tile)

    def hidden_units(dx, h):
        m_all[h].arrived(dx)

        def step(i, carry):
            cols = columns(i)
            z = jnp.dot(block(mixed, dx, h), w[:, cols], preferred_element_type=f32)
            z = z + bias_row[:, cols]
            t = jnp.tanh(0.5 * z)
            sg = 0.5 + 0.5 * t
            slope = 0.25 * (1.0 - t * t)
            first = sg + z * slope
            second = slope * (2.0 - z * t)
            by = head_row[:, cols]
            d1[dx, h, :, cols] = first
            d2[dx, h, :, cols] = second * by
            u[dx, h, :, cols] = (first * by).astype(bf16)
            return carry

        lax.fori_loop(0, hidden // tile, step, 0)

    def pair_copy(h):
        return pltpu.make_async_remote_copy(
            src_ref=to_pair.at[h], dst_ref=from_pair.at[h], send_sem=p_send.at[h],
            recv_sem=p_recv.at[h], device_id=dev(0, 0, 1), device_id_type=MESH,
        )

    def z_copy(h, k):
        return pltpu.make_async_remote_copy(
            src_ref=to_z.at[h, k], dst_ref=from_z.at[h, k], send_sem=z_send.at[h, k],
            recv_sem=z_recv.at[h, k], device_id=dev(0, k, 0), device_id_type=MESH,
        )

    def input_gradient(h):
        def step(i, carry):
            cols = columns(i)
            g = lax.dot_general(
                u[0, h], w[cols, :], (((1,), (1,)), ((), ())), preferred_element_type=f32
            ).reshape(nz, 2, rows, tile)
            for k in every:
                own[h, k, :, cols] = g[k, 0]
                to_pair[h, k, :, cols] = g[k, 1].astype(bf16)
            return carry

        lax.fori_loop(0, feats // tile, step, 0)
        pair_copy(h).start()

    def pair_sum(h):
        pair_copy(h).wait_recv()
        for k in others + (0,):
            both = own[h, k] + from_pair[h, k].astype(f32)
            if k:
                to_z[h, k] = both.astype(bf16)
                z_copy(h, k).start()
            else:
                own[h, 0] = both

    def scale_rows(h):
        g = own[h, 0]
        for k in others:
            z_copy(h, k).wait_recv()
            g = g + from_z[h, k].astype(f32)
        norm = jnp.sqrt(jnp.sum(g * g, axis=1, keepdims=True) + 1e-06)
        big[h, 0, 0, 0] = (20.0 * (norm - 1.0) / norm * g).astype(bf16)
        b_all[h].start()
        return jnp.sum((norm - 1.0) ** 2, axis=0, keepdims=True)

    def weight_terms(dx, h, start=False):
        b_all[h].arrived(dx)
        mine = pl.ds(pl.multiple_of(dp * part, 128), part)
        for j, held in enumerate((mixed, big)):
            lhs[j] = held[h, dx, :, :, :, mine].reshape(lot, part).T

        def step(i, carry):
            cols = columns(i)
            p = jnp.dot(block(big, dx, h), w[:, cols], preferred_element_type=f32)
            dz = p * d2[dx, h, :, cols]
            ph = p * d1[dx, h, :, cols]
            add_bias = jnp.sum(dz.reshape(lot // 8, 8, tile), axis=0)
            add_head = jnp.sum(ph.reshape(lot // 8, 8, tile), axis=0)
            if h == 0:
                sum_bias[dx, :, cols] = add_bias
                sum_head[dx, :, cols] = add_head
            else:
                sum_bias[dx, :, cols] += add_bias
                sum_head[dx, :, cols] += add_head
            term = jnp.dot(lhs[0], dz.astype(bf16), preferred_element_type=f32)
            term = term + jnp.dot(lhs[1], u[dx, h, :, cols], preferred_element_type=f32)
            if start:
                out[:, cols] = term
            else:
                out[:, cols] += term
            return carry

        lax.fori_loop(0, hidden // tile, step, 0)

    hops = [dev(0, 0, 1)]
    bit = 1
    while bit < nz:
        hops.append(dev(0, bit, 0))
        bit *= 2
    hops += [dev(1, 0, 0), dev(2, 0, 0)]

    def loss_copy(i):
        return pltpu.make_async_remote_copy(
            src_ref=loss.at[i], dst_ref=loss_in.at[i], send_sem=l_send.at[i],
            recv_sem=l_recv.at[i], device_id=hops[i], device_id_type=MESH,
        )

    state = [0]

    def loss_step():
        i = state[0]
        if i < len(hops):
            loss_copy(i).wait_recv()
            loss[i + 1] = loss[i] + loss_in[i]
            if i + 1 < len(hops):
                loss_copy(i + 1).start()
            state[0] = i + 1

    m_all[0].start()
    m_all[1].start()
    load_w.wait()
    m_all[0].spread(*others)
    hidden_units(0, 0)
    input_gradient(0)
    m_all[0].turn(*every)
    hidden_units(1, 0)
    pair_sum(0)
    m_all[1].spread(*others)
    hidden_units(0, 1)
    input_gradient(1)
    m_all[0].last(*every)
    hidden_units(2, 0)
    pair_sum(1)
    miss = scale_rows(0)
    hidden_units(3, 0)
    b_all[0].spread(1)
    m_all[1].turn(*every)
    hidden_units(1, 1)
    b_all[0].spread(*others[1:])
    hidden_units(2, 1)
    miss = miss + scale_rows(1)
    loss[0] = jnp.broadcast_to(miss, loss.shape[1:])
    loss_copy(0).start()
    m_all[1].last(*every)
    b_all[0].turn(0, 1)
    hidden_units(3, 1)
    loss_step()

    b_all[0].turn(*every[2:])
    b_all[1].spread(1)
    weight_terms(0, 0, True)
    loss_step()
    b_all[1].spread(*others[1:])
    weight_terms(1, 0)
    loss_step()
    b_all[0].last(*every)
    b_all[1].turn(0, 1)
    weight_terms(2, 0)
    loss_step()
    b_all[1].turn(*every[2:])
    weight_terms(3, 0)
    loss_step()
    weight_terms(0, 1)
    b_all[1].last(*every)
    weight_terms(1, 1)
    weight_terms(2, 1)
    weight_terms(3, 1)
    while state[0] < len(hops):
        loss_step()

    for ref, sums in ((out_bias, sum_bias), (out_head, sum_head)):
        whole = (sums[0] + sums[1]) + (sums[2] + sums[3])
        ref[...] = jnp.sum(whole, axis=0, keepdims=True).reshape(hidden)
    out_pen[0, 0] = (10.0 * loss[len(hops)] / total_rows)[0, 0]

    for h in range(2):
        m_all[h].finish()
        b_all[h].finish()
        pair_copy(h).wait_send()
        for k in others:
            z_copy(h, k).wait_send()
    for i in range(len(hops)):
        loss_copy(i).wait_send()


def scratch_of(rows, feats, hidden, part, nz):
    f32, bf16 = jnp.float32, jnp.bfloat16
    hops = nz.bit_length() + 2
    lot = nz * rows
    held = [
        ((feats, hidden), bf16),
        ((2, 4, nz, 2, rows // 2, feats), bf16),
        ((2, 4, nz, 2, rows // 2, feats), bf16),
        ((4, 2, lot, hidden), bf16),
        ((4, 2, lot, hidden), f32),
        ((4, 2, lot, hidden), f32),
        ((2, nz, rows // 2, feats), f32),
        ((2, part, lot), bf16),
        ((2, nz, rows // 2, feats), bf16),
        ((2, nz, rows // 2, feats), bf16),
        ((2, nz, rows // 2, feats), bf16),
        ((2, nz, rows // 2, feats), bf16),
        ((4, 8, hidden), f32),
        ((4, 8, hidden), f32),
        ((hops + 1, 8, 128), f32),
        ((hops + 1, 8, 128), f32),
        ((1, hidden), f32),
        ((1, hidden), f32),
    ]
    moves = nz - 1 + 8 * nz
    sems = [(), (2, moves), (2, moves), (2, moves), (2, moves), (2,), (2,), (2, nz), (2, nz), (hops,), (hops,)]
    return held, sems


def solution(mesh):
    placed = (
        P(("dp", "tensor"), None),
        P(("dp", "tensor"), None),
        P(("dp", "tensor")),
        P(None, "tensor"),
        P("tensor"),
        P("tensor"),
    )
    groups, members = mesh.shape["dp"], mesh.shape["tensor"]
    nz = members // 2

    def body(real_feats, fake_feats, mix_num, w_first, bias, head):
        rows, feats = real_feats.shape
        hidden = w_first.shape[1]
        part = feats // groups
        held, sems = scratch_of(rows, feats, hidden, part, max(nz, 2))
        size = part * hidden * 4
        for shape, dtype in held:
            size += functools.reduce(lambda a, b: a * b, shape) * jnp.dtype(dtype).itemsize
        tile = next((t for t in (512, 256, 128) if hidden % t == 0 and feats % t == 0), 0)
        fits = (
            groups == 4 and members % 2 == 0 and nz >= 2 and nz & (nz - 1) == 0
            and tile and rows % 64 == 0 and part % 128 == 0 and size <= HELD_BYTES
        )
        if not fits:
            return local(real_feats, fake_feats, mix_num, w_first, bias, head)
        vmem = pl.BlockSpec(memory_space=pltpu.VMEM)
        total_rows = rows * groups * members
        grad_w, grad_bias, grad_head, pen = pl.pallas_call(
            functools.partial(kernel, nz, tile, total_rows),
            out_shape=(
                jax.ShapeDtypeStruct((part, hidden), jnp.float32),
                jax.ShapeDtypeStruct((hidden,), jnp.float32),
                jax.ShapeDtypeStruct((hidden,), jnp.float32),
                jax.ShapeDtypeStruct((1, 1), jnp.float32),
            ),
            in_specs=[vmem, vmem, vmem, pl.BlockSpec(memory_space=pl.ANY), vmem, vmem],
            out_specs=(vmem, vmem, vmem, pl.BlockSpec(memory_space=pltpu.SMEM)),
            scratch_shapes=[pltpu.VMEM(s, t) for s, t in held]
            + [pltpu.SemaphoreType.DMA(s) if s else pltpu.SemaphoreType.DMA for s in sems],
            compiler_params=pltpu.CompilerParams(
                collective_id=0, has_side_effects=True, vmem_limit_bytes=VMEM_BYTES
            ),
        )(real_feats, fake_feats, mix_num, w_first, bias, head)
        return (grad_w, grad_bias, grad_head, pen.reshape(()))

    return jax.shard_map(
        body,
        mesh=mesh,
        in_specs=placed,
        out_specs=(P("dp", "tensor"), P("tensor"), P("tensor"), P()),
        check_vma=False,
    )
```

time: 111 us -> 101 us (0.910); the launches traced: 110 us -> 101 us
  local copies, waits for them, and re-layouts: 8.36 us -> 4.44 us
  Pallas kernels: 98.2 us -> 94.5 us
  other arithmetic: 2.62 us -> 0 us
  between operations: 0.64 us -> 2.35 us
    broadcast_in_dim x3 -> x0, local copies, waits for them, and re-layouts: 3.95 us -> none  [the longest x1 1.36 us: body(): mix_num[:, None]]
    pallas_call x1, Pallas kernels: 98.2 us -> 94.5 us  [body(): pl.pallas_call(functools.partial(kernel, nz, tile, total_rows), out_shape...]
    pallas_call x2 -> x0, other arithmetic: 2.62 us -> none  [body(): pl.pallas_call(functools.partial(kernel, nz, tile, total_rows), out_shape...]
    unnamed x1 -> x7, local copies, waits for them, and re-layouts: 3.22 us -> 4.44 us
    slice x1 -> x0, local copies, waits for them, and re-layouts: 1.19 us -> none  [body(): return (grad_w, grad_bias[0], grad_head[0], pen[0, 0])]
where the time goes in v2:
time: 101 us
  Pallas kernels  94.5 us (94%)
  local copies, waits for them, and re-layouts  4.44 us (4%)
  between operations  2.35 us (2%)
    pallas_call x1, Pallas kernels, body(): pl.pallas_call(functools.partial(kernel, nz, tile, total_rows), out_shape...  94.5 us
    unnamed x7, local copies, waits for them, and re-layouts  4.44 us

profile of v2, /device:TPU:0, one launch (start us, length us, event | category | flops | bytes accessed | tf_op | source)
XLA Modules:
  0.0 101.3 jit_solution(13208706260650885133)
XLA Ops:
  0.6 94.5 %shard_map.93 = (f32[384,1536]{1,0:T(8,128)}, f32[1536]{0:T(1024)}, f32[1536]{0:T(1024)}, f32[1,1]{1,0:T(1,128)}) custom-call(bf16[64,1536]{1,0:T(8,128)(2,1)} %real.1, bf16[64,1536]{1,0:T(8,128)(2,1)} %fake.1, s32[64]{0:T(128)} %mix.1, bf16[1536,1536]{1,0:T(8,128)(2,1)} %w_hbm.1, f32[1536]{0:T(1024)} %bias.1, f32[1536]{0:T(1024)} %head.1), custom_call_target="tpu_custom_call" | custom-call | tf_op jit(solution)/shard_map/pallas_call | solution.py:424
  95.1 0.0 copy-start.1
  95.2 0.0 copy-start
  95.2 3.2 %copy.14 = f32[384,1536]{1,0:T(8,128)} copy(f32[384,1536]{1,0:T(8,128)} %get-tuple-element.16) | data formatting | bytes 4718592
  98.4 0.0 copy-done.1
  98.4 0.6 copy.15
  99.0 0.0 copy-done
  99.0 0.6 copy.16
Async XLA Ops:
  95.1 3.3 %copy-start.1 = (f32[1536]{0:T(1024)S(1)}, f32[1536]{0:T(1024)}, u32[]{:S(2)}) copy-start(f32[1536]{0:T(1024)} %get-tuple-element.17) | copy-start | bytes 18436
  95.2 3.8 %copy-start = (f32[1536]{0:T(1024)S(1)}, f32[1536]{0:T(1024)}, u32[]{:S(2)}) copy-start(f32[1536]{0:T(1024)} %get-tuple-element.18) | copy-start | bytes 18436

commit v3 on v2

--- a/solution.py
+++ b/solution.py
@@ -118,10 +118,6 @@
             self.copy(("d", 1, k)).wait_recv()
             self.copy(("c", 3, k)).start()
 
-    def arrived(self, dx):
-        for k in range(self.nz):
-            self.copy(("c", dx, k)).wait_recv()
-
     def finish(self):
         for name in self.names:
             self.copy(name).wait_send()
@@ -174,14 +170,21 @@
     def block(held, dx, h):
         return held[h, dx].reshape(lot, feats)
 
-    def columns(i):
-        return pl.ds(pl.multiple_of(i * tile, tile), tile)
+    def arrived(held, send, recv, dx, h):
+        for k in every:
+            i = nz - 1 + dx * nz + k
+            pltpu.make_async_remote_copy(
+                src_ref=held.at[h, dx, k, 0], dst_ref=held.at[h, dx, k, 1],
+                send_sem=send.at[h, i], recv_sem=recv.at[h, i],
+                device_id=dev(0, 0, 1), device_id_type=MESH,
+            ).wait_recv()
+
+    def tiles(extent):
+        return [pl.ds(i, tile) for i in range(0, extent, tile)]
 
     def hidden_units(dx, h):
-        m_all[h].arrived(dx)
-
-        def step(i, carry):
-            cols = columns(i)
+        arrived(mixed, m_send, m_recv, dx, h)
+        for cols in tiles(hidden):
             z = jnp.dot(block(mixed, dx, h), w[:, cols], preferred_element_type=f32)
             z = z + bias_row[:, cols]
             t = jnp.tanh(0.5 * z)
@@ -193,9 +196,6 @@
             d1[dx, h, :, cols] = first
             d2[dx, h, :, cols] = second * by
             u[dx, h, :, cols] = (first * by).astype(bf16)
-            return carry
-
-        lax.fori_loop(0, hidden // tile, step, 0)
 
     def pair_copy(h):
         return pltpu.make_async_remote_copy(
@@ -210,17 +210,13 @@
         )
 
     def input_gradient(h):
-        def step(i, carry):
-            cols = columns(i)
+        for cols in tiles(feats):
             g = lax.dot_general(
                 u[0, h], w[cols, :], (((1,), (1,)), ((), ())), preferred_element_type=f32
             ).reshape(nz, 2, rows, tile)
             for k in every:
                 own[h, k, :, cols] = g[k, 0]
                 to_pair[h, k, :, cols] = g[k, 1].astype(bf16)
-            return carry
-
-        lax.fori_loop(0, feats // tile, step, 0)
         pair_copy(h).start()
 
     def pair_sum(h):
@@ -243,34 +239,20 @@
         b_all[h].start()
         return jnp.sum((norm - 1.0) ** 2, axis=0, keepdims=True)
 
-    def weight_terms(dx, h, start=False):
-        b_all[h].arrived(dx)
+    def weight_terms(dx, h):
+        arrived(big, b_send, b_recv, dx, h)
         mine = pl.ds(pl.multiple_of(dp * part, 128), part)
         for j, held in enumerate((mixed, big)):
             lhs[j] = held[h, dx, :, :, :, mine].reshape(lot, part).T
-
-        def step(i, carry):
-            cols = columns(i)
+        for cols in tiles(hidden):
             p = jnp.dot(block(big, dx, h), w[:, cols], preferred_element_type=f32)
             dz = p * d2[dx, h, :, cols]
             ph = p * d1[dx, h, :, cols]
-            add_bias = jnp.sum(dz.reshape(lot // 8, 8, tile), axis=0)
-            add_head = jnp.sum(ph.reshape(lot // 8, 8, tile), axis=0)
-            if h == 0:
-                sum_bias[dx, :, cols] = add_bias
-                sum_head[dx, :, cols] = add_head
-            else:
-                sum_bias[dx, :, cols] += add_bias
-                sum_head[dx, :, cols] += add_head
+            sum_bias[h, dx, :, cols] = jnp.sum(dz.reshape(lot // 8, 8, tile), axis=0)
+            sum_head[h, dx, :, cols] = jnp.sum(ph.reshape(lot // 8, 8, tile), axis=0)
             term = jnp.dot(lhs[0], dz.astype(bf16), preferred_element_type=f32)
             term = term + jnp.dot(lhs[1], u[dx, h, :, cols], preferred_element_type=f32)
-            if start:
-                out[:, cols] = term
-            else:
-                out[:, cols] += term
-            return carry
-
-        lax.fori_loop(0, hidden // tile, step, 0)
+            out[:, cols] += term
 
     hops = [dev(0, 0, 1)]
     bit = 1
@@ -285,71 +267,90 @@
             recv_sem=l_recv.at[i], device_id=hops[i], device_id_type=MESH,
         )
 
-    state = [0]
-
-    def loss_step():
-        i = state[0]
-        if i < len(hops):
-            loss_copy(i).wait_recv()
-            loss[i + 1] = loss[i] + loss_in[i]
-            if i + 1 < len(hops):
-                loss_copy(i + 1).start()
-            state[0] = i + 1
+    def loss_step(i):
+        loss_copy(i).wait_recv()
+        loss[i + 1] = loss[i] + loss_in[i]
+        if i + 1 < len(hops):
+            loss_copy(i + 1).start()
 
     m_all[0].start()
     m_all[1].start()
     load_w.wait()
     m_all[0].spread(*others)
-    hidden_units(0, 0)
-    input_gradient(0)
-    m_all[0].turn(*every)
-    hidden_units(1, 0)
-    pair_sum(0)
-    m_all[1].spread(*others)
-    hidden_units(0, 1)
-    input_gradient(1)
-    m_all[0].last(*every)
-    hidden_units(2, 0)
-    pair_sum(1)
-    miss = scale_rows(0)
-    hidden_units(3, 0)
-    b_all[0].spread(1)
-    m_all[1].turn(*every)
-    hidden_units(1, 1)
-    b_all[0].spread(*others[1:])
-    hidden_units(2, 1)
-    miss = miss + scale_rows(1)
-    loss[0] = jnp.broadcast_to(miss, loss.shape[1:])
-    loss_copy(0).start()
-    m_all[1].last(*every)
-    b_all[0].turn(0, 1)
-    hidden_units(3, 1)
-    loss_step()
-
-    b_all[0].turn(*every[2:])
-    b_all[1].spread(1)
-    weight_terms(0, 0, True)
-    loss_step()
-    b_all[1].spread(*others[1:])
-    weight_terms(1, 0)
-    loss_step()
-    b_all[0].last(*every)
-    b_all[1].turn(0, 1)
-    weight_terms(2, 0)
-    loss_step()
-    b_all[1].turn(*every[2:])
-    weight_terms(3, 0)
-    loss_step()
-    weight_terms(0, 1)
-    b_all[1].last(*every)
-    weight_terms(1, 1)
-    weight_terms(2, 1)
-    weight_terms(3, 1)
-    while state[0] < len(hops):
-        loss_step()
+
+    def after_hidden(n):
+        if n == 0:
+            m_all[0].turn(*every)
+        elif n == 1:
+            pair_sum(0)
+            m_all[1].spread(*others)
+        elif n == 2:
+            m_all[0].last(*every)
+        elif n == 3:
+            pair_sum(1)
+            loss[0] = jnp.broadcast_to(scale_rows(0), loss.shape[1:])
+        elif n == 4:
+            b_all[0].spread(1)
+            m_all[1].turn(*every)
+        elif n == 5:
+            b_all[0].spread(*others[1:])
+        elif n == 6:
+            loss[0] += jnp.broadcast_to(scale_rows(1), loss.shape[1:])
+            loss_copy(0).start()
+            m_all[1].last(*every)
+            b_all[0].turn(*every[:2])
+        else:
+            loss_step(0)
+            b_all[0].turn(*every[2:])
+            b_all[1].spread(1)
+
+    order = ((0, 0), (1, 0), (0, 1), (2, 0), (3, 0), (1, 1), (2, 1), (3, 1))
+
+    def hidden_step(n, carry):
+        dx, h = n * 0, n * 0
+        for i, (group, half) in enumerate(order):
+            dx = jnp.where(n == i, group, dx)
+            h = jnp.where(n == i, half, h)
+        hidden_units(dx, h)
+
+        @pl.when(jnp.logical_or(n == 0, n == 2))
+        def _():
+            input_gradient(h)
+
+        for i in range(len(order)):
+            pl.when(n == i)(functools.partial(after_hidden, i))
+        return carry
+
+    lax.fori_loop(0, len(order), hidden_step, 0)
+
+    out[...] = jnp.zeros_like(out)
+
+    def before_weights(n):
+        if n == 0:
+            b_all[1].spread(*others[1:])
+        elif n == 2:
+            b_all[0].last(*every)
+            b_all[1].turn(*every[:2])
+        elif n == 3:
+            b_all[1].turn(*every[2:])
+        elif n == 5:
+            b_all[1].last(*every)
+        if n + 1 < len(hops):
+            loss_step(n + 1)
+
+    def weight_step(n, carry):
+        for i in range(len(order)):
+            pl.when(n == i)(functools.partial(before_weights, i))
+        weight_terms(lax.rem(n, 4), n // 4)
+        return carry
+
+    lax.fori_loop(0, len(order), weight_step, 0)
+    for i in range(len(order) + 1, len(hops)):
+        loss_step(i)
 
     for ref, sums in ((out_bias, sum_bias), (out_head, sum_head)):
-        whole = (sums[0] + sums[1]) + (sums[2] + sums[3])
+        part_sums = [sums[0, dx] + sums[1, dx] for dx in range(4)]
+        whole = (part_sums[0] + part_sums[1]) + (part_sums[2] + part_sums[3])
         ref[...] = jnp.sum(whole, axis=0, keepdims=True).reshape(hidden)
     out_pen[0, 0] = (10.0 * loss[len(hops)] / total_rows)[0, 0]
 
@@ -380,8 +381,8 @@
         ((2, nz, rows // 2, feats), bf16),
         ((2, nz, rows // 2, feats), bf16),
         ((2, nz, rows // 2, feats), bf16),
-        ((4, 8, hidden), f32),
-        ((4, 8, hidden), f32),
+        ((2, 4, 8, hidden), f32),
+        ((2, 4, 8, hidden), f32),
         ((hops + 1, 8, 128), f32),
         ((hops + 1, 8, 128), f32),
         ((1, hidden), f32),
@@ -412,7 +413,7 @@
         size = part * hidden * 4
         for shape, dtype in held:
             size += functools.reduce(lambda a, b: a * b, shape) * jnp.dtype(dtype).itemsize
-        tile = next((t for t in (512, 256, 128) if hidden % t == 0 and feats % t == 0), 0)
+        tile = next((t for t in (256, 128) if hidden % t == 0 and feats % t == 0), 0)
         fits = (
             groups == 4 and members % 2 == 0 and nz >= 2 and nz & (nz - 1) == 0
             and tile and rows % 64 == 0 and part % 128 == 0 and size <= HELD_BYTES

time: 101 us -> 109 us (1.079)
  Pallas kernels: 94.5 us -> 103 us
    pallas_call x1, Pallas kernels: 94.5 us -> 103 us  [body(): pl.pallas_call(functools.partial(kernel, nz, tile, total_rows), out_shape...]
where the time goes in v3:
time: 109 us
  Pallas kernels  103 us (94%)
  local copies, waits for them, and re-layouts  4.44 us (4%)
  between operations  2.35 us (2%)
    pallas_call x1, Pallas kernels, body(): pl.pallas_call(functools.partial(kernel, nz, tile, total_rows), out_shape...  103 us
    unnamed x7, local copies, waits for them, and re-layouts  4.44 us

profile of v3, /device:TPU:0, one launch (start us, length us, event | category | flops | bytes accessed | tf_op | source)
XLA Modules:
  0.0 109.3 jit_solution(13887204569251696960)
XLA Ops:
  0.6 102.5 %shard_map.93 = (f32[384,1536]{1,0:T(8,128)}, f32[1536]{0:T(1024)}, f32[1536]{0:T(1024)}, f32[1,1]{1,0:T(1,128)}) custom-call(bf16[64,1536]{1,0:T(8,128)(2,1)} %real.1, bf16[64,1536]{1,0:T(8,128)(2,1)} %fake.1, s32[64]{0:T(128)} %mix.1, bf16[1536,1536]{1,0:T(8,128)(2,1)} %w_hbm.1, f32[1536]{0:T(1024)} %bias.1, f32[1536]{0:T(1024)} %head.1), custom_call_target="tpu_custom_call" | custom-call | tf_op jit(solution)/shard_map/pallas_call | solution.py:425
  103.2 0.0 copy-start.1
  103.2 0.0 copy-start
  103.2 3.2 %copy.14 = f32[384,1536]{1,0:T(8,128)} copy(f32[384,1536]{1,0:T(8,128)} %get-tuple-element.16) | data formatting | bytes 4718592
  106.4 0.0 copy-done.1
  106.4 0.6 copy.15
  107.0 0.0 copy-done
  107.0 0.6 copy.16
Async XLA Ops:
  103.2 3.3 %copy-start.1 = (f32[1536]{0:T(1024)S(1)}, f32[1536]{0:T(1024)}, u32[]{:S(2)}) copy-start(f32[1536]{0:T(1024)} %get-tuple-element.17) | copy-start | bytes 18436
  103.2 3.8 %copy-start = (f32[1536]{0:T(1024)S(1)}, f32[1536]{0:T(1024)}, u32[]{:S(2)}) copy-start(f32[1536]{0:T(1024)} %get-tuple-element.18) | copy-start | bytes 18436

commit v4 on v3

--- a/solution.py
+++ b/solution.py
@@ -8,8 +8,8 @@
 from jax.sharding import PartitionSpec as P
 
 MESH = pl.DeviceIdType.MESH
-VMEM_BYTES = 62 * 2**20
-HELD_BYTES = 58 * 2**20
+VMEM_BYTES = 63 * 2**20
+HELD_BYTES = 61 * 2**20
 
 
 def row_contract(left, right):
@@ -127,8 +127,8 @@
     nz, tile, total_rows,
     real, fake, mix, w_hbm, bias, head,
     out, out_bias, out_head, out_pen,
-    w, mixed, big, u, d1, d2, own, lhs, to_pair, from_pair, to_z, from_z,
-    sum_bias, sum_head, loss, loss_in, bias_row, head_row,
+    w, w_t, mixed, big, u, d1, d2, own, to_pair, from_pair, to_z, from_z,
+    sums, loss, loss_in, bias_col, head_col,
     w_sem, m_send, m_recv, b_send, b_recv, p_send, p_recv, z_send, z_recv, l_send, l_recv,
 ):
     f32, bf16 = jnp.float32, jnp.bfloat16
@@ -138,7 +138,7 @@
     rows = real.shape[0] // 2
     lot = 2 * nz * rows
     hidden = w.shape[1]
-    part = out.shape[0]
+    part = out.shape[1]
     every, others = tuple(range(nz)), tuple(range(1, nz))
 
     def dev(dx, zx, cc):
@@ -160,8 +160,6 @@
     rows_in = (real_f + coef * (fake[...].astype(f32) - real_f)).astype(bf16)
     for h in range(2):
         mixed[h, 0, 0, 0] = rows_in[h * rows:(h + 1) * rows]
-    bias_row[...] = bias[...].reshape(1, hidden)
-    head_row[...] = head[...].reshape(1, hidden)
     pl.semaphore_wait(barrier, len(partners))
 
     m_all = [Gather(mixed.at[h], nz, m_send.at[h], m_recv.at[h], dev) for h in range(2)]
@@ -179,23 +177,31 @@
                 device_id=dev(0, 0, 1), device_id_type=MESH,
             ).wait_recv()
 
-    def tiles(extent):
-        return [pl.ds(i, tile) for i in range(0, extent, tile)]
+    def tiles(extent, size=tile):
+        return [pl.ds(i, size) for i in range(0, extent, size)]
+
+    def across(col, units):
+        return jnp.concatenate([col[units, :]] * (lot // 128), axis=1)
+
+    def product(left, right):
+        return lax.dot_general(
+            left, right, (((1,), (1,)), ((), ())), preferred_element_type=f32
+        )
 
     def hidden_units(dx, h):
         arrived(mixed, m_send, m_recv, dx, h)
-        for cols in tiles(hidden):
-            z = jnp.dot(block(mixed, dx, h), w[:, cols], preferred_element_type=f32)
-            z = z + bias_row[:, cols]
+        for units in tiles(hidden):
+            z = product(w_t[units, :], block(mixed, dx, h))
+            z = z + across(bias_col, units)
             t = jnp.tanh(0.5 * z)
             sg = 0.5 + 0.5 * t
             slope = 0.25 * (1.0 - t * t)
             first = sg + z * slope
             second = slope * (2.0 - z * t)
-            by = head_row[:, cols]
-            d1[dx, h, :, cols] = first
-            d2[dx, h, :, cols] = second * by
-            u[dx, h, :, cols] = (first * by).astype(bf16)
+            by = across(head_col, units)
+            d1[dx, h, units, :] = first
+            d2[dx, h, units, :] = second * by
+            u[dx, h, units, :] = (first * by).astype(bf16)
 
     def pair_copy(h):
         return pltpu.make_async_remote_copy(
@@ -211,9 +217,8 @@
 
     def input_gradient(h):
         for cols in tiles(feats):
-            g = lax.dot_general(
-                u[0, h], w[cols, :], (((1,), (1,)), ((), ())), preferred_element_type=f32
-            ).reshape(nz, 2, rows, tile)
+            g = jnp.dot(w[cols, :], u[0, h], preferred_element_type=f32).T
+            g = g.reshape(nz, 2, rows, tile)
             for k in every:
                 own[h, k, :, cols] = g[k, 0]
                 to_pair[h, k, :, cols] = g[k, 1].astype(bf16)
@@ -242,17 +247,20 @@
     def weight_terms(dx, h):
         arrived(big, b_send, b_recv, dx, h)
         mine = pl.ds(pl.multiple_of(dp * part, 128), part)
-        for j, held in enumerate((mixed, big)):
-            lhs[j] = held[h, dx, :, :, :, mine].reshape(lot, part).T
-        for cols in tiles(hidden):
-            p = jnp.dot(block(big, dx, h), w[:, cols], preferred_element_type=f32)
-            dz = p * d2[dx, h, :, cols]
-            ph = p * d1[dx, h, :, cols]
-            sum_bias[h, dx, :, cols] = jnp.sum(dz.reshape(lot // 8, 8, tile), axis=0)
-            sum_head[h, dx, :, cols] = jnp.sum(ph.reshape(lot // 8, 8, tile), axis=0)
-            term = jnp.dot(lhs[0], dz.astype(bf16), preferred_element_type=f32)
-            term = term + jnp.dot(lhs[1], u[dx, h, :, cols], preferred_element_type=f32)
-            out[:, cols] += term
+        mixed_part = mixed[h, dx, :, :, :, mine].reshape(lot, part)
+        big_part = big[h, dx, :, :, :, mine].reshape(lot, part)
+        for units in tiles(hidden):
+            p = product(w_t[units, :], block(big, dx, h))
+            dz = p * d2[dx, h, units, :]
+            ph = p * d1[dx, h, units, :]
+            lane = lax.broadcasted_iota(jnp.int32, (tile, 128), 1)
+            row = sums[units, :]
+            row = jnp.where(lane == 2 * dx + h, jnp.sum(dz, axis=1, keepdims=True), row)
+            row = jnp.where(lane == 8 + 2 * dx + h, jnp.sum(ph, axis=1, keepdims=True), row)
+            sums[units, :] = row
+            term = jnp.dot(dz.astype(bf16), mixed_part, preferred_element_type=f32)
+            term = term + jnp.dot(u[dx, h, units, :], big_part, preferred_element_type=f32)
+            out[units, :] += term
 
     hops = [dev(0, 0, 1)]
     bit = 1
@@ -275,7 +283,11 @@
 
     m_all[0].start()
     m_all[1].start()
+    for ref, col in ((bias, bias_col), (head, head_col)):
+        col[...] = jnp.broadcast_to(ref[...].reshape(1, hidden), (128, hidden)).T
     load_w.wait()
+    for cols in tiles(hidden, 256):
+        w_t[cols, :] = w[:, cols].T
     m_all[0].spread(*others)
 
     def after_hidden(n):
@@ -324,6 +336,7 @@
     lax.fori_loop(0, len(order), hidden_step, 0)
 
     out[...] = jnp.zeros_like(out)
+    sums[...] = jnp.zeros_like(sums)
 
     def before_weights(n):
         if n == 0:
@@ -348,10 +361,10 @@
     for i in range(len(order) + 1, len(hops)):
         loss_step(i)
 
-    for ref, sums in ((out_bias, sum_bias), (out_head, sum_head)):
-        part_sums = [sums[0, dx] + sums[1, dx] for dx in range(4)]
-        whole = (part_sums[0] + part_sums[1]) + (part_sums[2] + part_sums[3])
-        ref[...] = jnp.sum(whole, axis=0, keepdims=True).reshape(hidden)
+    by_lot = sums[...].T
+    for ref, first in ((out_bias, 0), (out_head, 8)):
+        group = [by_lot[first + i:first + i + 1] + by_lot[first + i + 1:first + i + 2] for i in (0, 2, 4, 6)]
+        ref[...] = ((group[0] + group[1]) + (group[2] + group[3])).reshape(hidden)
     out_pen[0, 0] = (10.0 * loss[len(hops)] / total_rows)[0, 0]
 
     for h in range(2):
@@ -370,23 +383,22 @@
     lot = nz * rows
     held = [
         ((feats, hidden), bf16),
+        ((hidden, feats), bf16),
         ((2, 4, nz, 2, rows // 2, feats), bf16),
         ((2, 4, nz, 2, rows // 2, feats), bf16),
-        ((4, 2, lot, hidden), bf16),
-        ((4, 2, lot, hidden), f32),
-        ((4, 2, lot, hidden), f32),
+        ((4, 2, hidden, lot), bf16),
+        ((4, 2, hidden, lot), f32),
+        ((4, 2, hidden, lot), f32),
         ((2, nz, rows // 2, feats), f32),
-        ((2, part, lot), bf16),
         ((2, nz, rows // 2, feats), bf16),
         ((2, nz, rows // 2, feats), bf16),
         ((2, nz, rows // 2, feats), bf16),
         ((2, nz, rows // 2, feats), bf16),
-        ((2, 4, 8, hidden), f32),
-        ((2, 4, 8, hidden), f32),
+        ((hidden, 128), f32),
         ((hops + 1, 8, 128), f32),
         ((hops + 1, 8, 128), f32),
-        ((1, hidden), f32),
-        ((1, hidden), f32),
+        ((hidden, 128), f32),
+        ((hidden, 128), f32),
     ]
     moves = nz - 1 + 8 * nz
     sems = [(), (2, moves), (2, moves), (2, moves), (2, moves), (2,), (2,), (2, nz), (2, nz), (hops,), (hops,)]
@@ -413,10 +425,10 @@
         size = part * hidden * 4
         for shape, dtype in held:
             size += functools.reduce(lambda a, b: a * b, shape) * jnp.dtype(dtype).itemsize
-        tile = next((t for t in (256, 128) if hidden % t == 0 and feats % t == 0), 0)
+        tile = next((t for t in (768, 512, 256) if hidden % t == 0 and feats % t == 0), 0)
         fits = (
             groups == 4 and members % 2 == 0 and nz >= 2 and nz & (nz - 1) == 0
-            and tile and rows % 64 == 0 and part % 128 == 0 and size <= HELD_BYTES
+            and tile and rows % 64 == 0 and nz * rows % 128 == 0 and part % 128 == 0 and size <= HELD_BYTES
         )
         if not fits:
             return local(real_feats, fake_feats, mix_num, w_first, bias, head)
@@ -425,7 +437,7 @@
         grad_w, grad_bias, grad_head, pen = pl.pallas_call(
             functools.partial(kernel, nz, tile, total_rows),
             out_shape=(
-                jax.ShapeDtypeStruct((part, hidden), jnp.float32),
+                jax.ShapeDtypeStruct((hidden, part), jnp.float32),
                 jax.ShapeDtypeStruct((hidden,), jnp.float32),
                 jax.ShapeDtypeStruct((hidden,), jnp.float32),
                 jax.ShapeDtypeStruct((1, 1), jnp.float32),
@@ -438,7 +450,7 @@
                 collective_id=0, has_side_effects=True, vmem_limit_bytes=VMEM_BYTES
             ),
         )(real_feats, fake_feats, mix_num, w_first, bias, head)
-        return (grad_w, grad_bias, grad_head, pen.reshape(()))
+        return (grad_w.T, grad_bias, grad_head, pen.reshape(()))
 
     return jax.shard_map(
         body,

time: 109 us -> 107 us (0.982)
  Pallas kernels: 103 us -> 100 us
    pallas_call x1, Pallas kernels: 103 us -> 100 us  [body(): pl.pallas_call(functools.partial(kernel, nz, tile, total_rows), out_shape...]
where the time goes in v4:
time: 107 us
  Pallas kernels  100 us (93%)
  local copies, waits for them, and re-layouts  4.26 us (4%)
  between operations  2.35 us (2%)
    pallas_call x1, Pallas kernels, body(): pl.pallas_call(functools.partial(kernel, nz, tile, total_rows), out_shape...  100 us
    unnamed x7, local copies, waits for them, and re-layouts  4.26 us

profile of v4, /device:TPU:0, one launch (start us, length us, event | category | flops | bytes accessed | tf_op | source)
XLA Modules:
  0.0 106.6 jit_solution(8877518529762655506)
XLA Ops:
  0.6 100.0 %shard_map.93 = (f32[1536,384]{1,0:T(8,128)}, f32[1536]{0:T(1024)}, f32[1536]{0:T(1024)}, f32[1,1]{1,0:T(1,128)}) custom-call(bf16[64,1536]{1,0:T(8,128)(2,1)} %real.1, bf16[64,1536]{1,0:T(8,128)(2,1)} %fake.1, s32[64]{0:T(128)} %mix.1, bf16[1536,1536]{1,0:T(8,128)(2,1)} %w_hbm.1, f32[1536]{0:T(1024)} %bias.1, f32[1536]{0:T(1024)} %head.1), custom_call_target="tpu_custom_call" | custom-call | tf_op jit(solution)/shard_map/pallas_call | solution.py:437
  100.6 0.0 copy-start.1
  100.6 0.0 copy-start
  100.6 3.1 %copy.10 = f32[384,1536]{1,0:T(8,128)} copy(f32[384,1536]{0,1:T(8,128)} %bitcast.2) | data formatting | bytes 4718592
  103.7 0.0 copy-done.1
  103.7 0.6 copy.14
  104.3 0.0 copy-done
  104.3 0.6 copy.15
Async XLA Ops:
  100.6 3.1 %copy-start.1 = (f32[1536]{0:T(1024)S(1)}, f32[1536]{0:T(1024)}, u32[]{:S(2)}) copy-start(f32[1536]{0:T(1024)} %get-tuple-element.21) | copy-start | bytes 18436
  100.6 3.7 %copy-start = (f32[1536]{0:T(1024)S(1)}, f32[1536]{0:T(1024)}, u32[]{:S(2)}) copy-start(f32[1536]{0:T(1024)} %get-tuple-element.22) | copy-start | bytes 18436

commit v5 on v4

--- a/solution.py
+++ b/solution.py
@@ -178,7 +178,14 @@
             ).wait_recv()
 
     def tiles(extent, size=tile):
-        return [pl.ds(i, size) for i in range(0, extent, size)]
+        def over(step):
+            def turn(i, carry):
+                step(pl.ds(pl.multiple_of(i * size, size), size))
+                return carry
+
+            lax.fori_loop(0, extent // size, turn, 0)
+
+        return over
 
     def across(col, units):
         return jnp.concatenate([col[units, :]] * (lot // 128), axis=1)
@@ -190,7 +197,8 @@
 
     def hidden_units(dx, h):
         arrived(mixed, m_send, m_recv, dx, h)
-        for units in tiles(hidden):
+        @tiles(hidden)
+        def _(units):
             z = product(w_t[units, :], block(mixed, dx, h))
             z = z + across(bias_col, units)
             t = jnp.tanh(0.5 * z)
@@ -216,12 +224,14 @@
         )
 
     def input_gradient(h):
-        for cols in tiles(feats):
+        @tiles(feats)
+        def _(cols):
             g = jnp.dot(w[cols, :], u[0, h], preferred_element_type=f32).T
             g = g.reshape(nz, 2, rows, tile)
             for k in every:
                 own[h, k, :, cols] = g[k, 0]
                 to_pair[h, k, :, cols] = g[k, 1].astype(bf16)
+
         pair_copy(h).start()
 
     def pair_sum(h):
@@ -249,7 +259,8 @@
         mine = pl.ds(pl.multiple_of(dp * part, 128), part)
         mixed_part = mixed[h, dx, :, :, :, mine].reshape(lot, part)
         big_part = big[h, dx, :, :, :, mine].reshape(lot, part)
-        for units in tiles(hidden):
+        @tiles(hidden)
+        def _(units):
             p = product(w_t[units, :], block(big, dx, h))
             dz = p * d2[dx, h, units, :]
             ph = p * d1[dx, h, units, :]
@@ -286,7 +297,8 @@
     for ref, col in ((bias, bias_col), (head, head_col)):
         col[...] = jnp.broadcast_to(ref[...].reshape(1, hidden), (128, hidden)).T
     load_w.wait()
-    for cols in tiles(hidden, 256):
+    @tiles(hidden, 256)
+    def _(cols):
         w_t[cols, :] = w[:, cols].T
     m_all[0].spread(*others)
 
@@ -425,7 +437,7 @@
         size = part * hidden * 4
         for shape, dtype in held:
             size += functools.reduce(lambda a, b: a * b, shape) * jnp.dtype(dtype).itemsize
-        tile = next((t for t in (768, 512, 256) if hidden % t == 0 and feats % t == 0), 0)
+        tile = next((t for t in (512, 256) if hidden % t == 0 and feats % t == 0), 0)
         fits = (
             groups == 4 and members % 2 == 0 and nz >= 2 and nz & (nz - 1) == 0
             and tile and rows % 64 == 0 and nz * rows % 128 == 0 and part % 128 == 0 and size <= HELD_BYTES

time: 107 us -> 108 us (level)
  Pallas kernels: 100 us -> 102 us
    pallas_call x1, Pallas kernels: 100 us -> 102 us  [body(): pl.pallas_call(functools.partial(kernel, nz, tile, total_rows), out_shape...]
where the time goes in v5:
time: 108 us
  Pallas kernels  102 us (94%)
  local copies, waits for them, and re-layouts  4.26 us (4%)
  between operations  2.35 us (2%)
    pallas_call x1, Pallas kernels, body(): pl.pallas_call(functools.partial(kernel, nz, tile, total_rows), out_shape...  102 us
    unnamed x7, local copies, waits for them, and re-layouts  4.26 us

profile of v5, /device:TPU:0, one launch (start us, length us, event | category | flops | bytes accessed | tf_op | source)
XLA Modules:
  0.0 108.1 jit_solution(16719787086222385769)
XLA Ops:
  0.6 101.5 %shard_map.93 = (f32[1536,384]{1,0:T(8,128)}, f32[1536]{0:T(1024)}, f32[1536]{0:T(1024)}, f32[1,1]{1,0:T(1,128)}) custom-call(bf16[64,1536]{1,0:T(8,128)(2,1)} %real.1, bf16[64,1536]{1,0:T(8,128)(2,1)} %fake.1, s32[64]{0:T(128)} %mix.1, bf16[1536,1536]{1,0:T(8,128)(2,1)} %w_hbm.1, f32[1536]{0:T(1024)} %bias.1, f32[1536]{0:T(1024)} %head.1), custom_call_target="tpu_custom_call" | custom-call | tf_op jit(solution)/shard_map/pallas_call | solution.py:449
  102.2 0.0 copy-start.1
  102.2 0.0 copy-start
  102.2 3.1 %copy.10 = f32[384,1536]{1,0:T(8,128)} copy(f32[384,1536]{0,1:T(8,128)} %bitcast.2) | data formatting | bytes 4718592
  105.2 0.0 copy-done.1
  105.2 0.6 copy.14
  105.8 0.0 copy-done
  105.8 0.6 copy.15
Async XLA Ops:
  102.2 3.1 %copy-start.1 = (f32[1536]{0:T(1024)S(1)}, f32[1536]{0:T(1024)}, u32[]{:S(2)}) copy-start(f32[1536]{0:T(1024)} %get-tuple-element.21) | copy-start | bytes 18436
  102.2 3.7 %copy-start = (f32[1536]{0:T(1024)S(1)}, f32[1536]{0:T(1024)}, u32[]{:S(2)}) copy-start(f32[1536]{0:T(1024)} %get-tuple-element.22) | copy-start | bytes 18436

commit v6 on v2

--- a/solution.py
+++ b/solution.py
@@ -64,10 +64,15 @@
     return index
 
 
+def relays(nz):
+    return {2: (3, 1)} if nz == 4 else {}
+
+
 class Gather:
     def __init__(self, held, nz, send, recv, dev):
         self.held, self.nz, self.dev = held, nz, dev
         self.send, self.recv = send, recv
+        self.via = relays(nz)
         self.names = (
             [("z", 0, k) for k in range(1, nz)]
             + [(kind, dx, k) for kind, dxs in (("c", range(4)), ("xy", (1, 2)), ("d", (0, 1)))
@@ -78,7 +83,10 @@
         kind, dx, k = name
         held, dev = self.held, self.dev
         half = held.shape[3] // 2
-        if kind == "z":
+        if kind == "z" and k in self.via:
+            held_at, step = self.via[k]
+            src, dst, to = held.at[0, held_at, 0], held.at[0, k, 0], dev(0, step, 0)
+        elif kind == "z":
             src, dst, to = held.at[0, 0, 0], held.at[0, k, 0], dev(0, k, 0)
         elif kind == "c":
             src, dst, to = held.at[dx, k, 0], held.at[dx, k, 1], dev(0, 0, 1)
@@ -95,13 +103,17 @@
 
     def start(self):
         for k in range(1, self.nz):
-            self.copy(("z", 0, k)).start()
+            if k not in self.via:
+                self.copy(("z", 0, k)).start()
         self.spread(0)
 
     def spread(self, *ks):
         for k in ks:
             if k:
                 self.copy(("z", 0, k)).wait_recv()
+            for later, (held_at, _) in self.via.items():
+                if held_at == k:
+                    self.copy(("z", 0, later)).start()
             for name in (("xy", 1, k), ("xy", 2, k), ("c", 0, k)):
                 self.copy(name).start()
 
@@ -143,7 +155,9 @@
     lot = 2 * nz * rows
     hidden = w.shape[1]
     part = out.shape[0]
-    every, others = tuple(range(nz)), tuple(range(1, nz))
+    via = relays(nz)
+    every = tuple(range(nz))
+    others = tuple(k for k in every[1:] if k not in via) + tuple(via)
 
     def dev(dx, zx, cc):
         return (flip(dp, dx), flip(z_at, zx) * 2 + flip(core, cc))
@@ -206,7 +220,8 @@
     def z_copy(h, k):
         return pltpu.make_async_remote_copy(
             src_ref=to_z.at[h, k], dst_ref=from_z.at[h, k], send_sem=z_send.at[h, k],
-            recv_sem=z_recv.at[h, k], device_id=dev(0, k, 0), device_id_type=MESH,
+            recv_sem=z_recv.at[h, k], device_id=dev(0, via[k][1] if k in via else k, 0),
+            device_id_type=MESH,
         )
 
     def input_gradient(h):
@@ -223,21 +238,30 @@
         lax.fori_loop(0, feats // tile, step, 0)
         pair_copy(h).start()
 
+    merged = {held_at: k for k, (held_at, _) in via.items()}
+
     def pair_sum(h):
         pair_copy(h).wait_recv()
-        for k in others + (0,):
+        for k in tuple(via) + tuple(k for k in every if k not in via):
             both = own[h, k] + from_pair[h, k].astype(f32)
-            if k:
+            if k in merged or k == 0:
+                own[h, k] = both
+            else:
                 to_z[h, k] = both.astype(bf16)
                 z_copy(h, k).start()
-            else:
-                own[h, 0] = both
+
+    def relay_sum(h):
+        for k, passed in merged.items():
+            z_copy(h, passed).wait_recv()
+            to_z[h, k] = (own[h, k] + from_z[h, passed].astype(f32)).astype(bf16)
+            z_copy(h, k).start()
 
     def scale_rows(h):
         g = own[h, 0]
         for k in others:
-            z_copy(h, k).wait_recv()
-            g = g + from_z[h, k].astype(f32)
+            if k not in via:
+                z_copy(h, k).wait_recv()
+                g = g + from_z[h, k].astype(f32)
         norm = jnp.sqrt(jnp.sum(g * g, axis=1, keepdims=True) + 1e-06)
         big[h, 0, 0, 0] = (20.0 * (norm - 1.0) / norm * g).astype(bf16)
         b_all[h].start()
@@ -305,15 +329,18 @@
     m_all[0].turn(*every)
     hidden_units(1, 0)
     pair_sum(0)
-    m_all[1].spread(*others)
+    m_all[1].spread(others[0])
+    relay_sum(0)
+    m_all[1].spread(*others[1:])
     hidden_units(0, 1)
     input_gradient(1)
     m_all[0].last(*every)
     hidden_units(2, 0)
     pair_sum(1)
     miss = scale_rows(0)
+    relay_sum(1)
     hidden_units(3, 0)
-    b_all[0].spread(1)
+    b_all[0].spread(others[0])
     m_all[1].turn(*every)
     hidden_units(1, 1)
     b_all[0].spread(*others[1:])
@@ -327,7 +354,7 @@
     loss_step()
 
     b_all[0].turn(*every[2:])
-    b_all[1].spread(1)
+    b_all[1].spread(others[0])
     weight_terms(0, 0, True)
     loss_step()
     b_all[1].spread(*others[1:])

time: 101 us -> 110 us (1.089)
  Pallas kernels: 94.5 us -> 103 us
    pallas_call x1, Pallas kernels: 94.5 us -> 103 us  [body(): pl.pallas_call(functools.partial(kernel, nz, tile, total_rows), out_shape...]
where the time goes in v6:
time: 110 us
  Pallas kernels  103 us (94%)
  local copies, waits for them, and re-layouts  4.44 us (4%)
  between operations  2.35 us (2%)
    pallas_call x1, Pallas kernels, body(): pl.pallas_call(functools.partial(kernel, nz, tile, total_rows), out_shape...  103 us
    unnamed x7, local copies, waits for them, and re-layouts  4.44 us

profile of v6, /device:TPU:0, one launch (start us, length us, event | category | flops | bytes accessed | tf_op | source)
XLA Modules:
  0.0 109.8 jit_solution(2948692884023519437)
XLA Ops:
  0.6 103.0 %shard_map.93 = (f32[384,1536]{1,0:T(8,128)}, f32[1536]{0:T(1024)}, f32[1536]{0:T(1024)}, f32[1,1]{1,0:T(1,128)}) custom-call(bf16[64,1536]{1,0:T(8,128)(2,1)} %real.1, bf16[64,1536]{1,0:T(8,128)(2,1)} %fake.1, s32[64]{0:T(128)} %mix.1, bf16[1536,1536]{1,0:T(8,128)(2,1)} %w_hbm.1, f32[1536]{0:T(1024)} %bias.1, f32[1536]{0:T(1024)} %head.1), custom_call_target="tpu_custom_call" | custom-call | tf_op jit(solution)/shard_map/pallas_call | solution.py:451
  103.7 0.0 copy-start.1
  103.7 0.0 copy-start
  103.7 3.2 %copy.14 = f32[384,1536]{1,0:T(8,128)} copy(f32[384,1536]{1,0:T(8,128)} %get-tuple-element.16) | data formatting | bytes 4718592
  106.9 0.0 copy-done.1
  106.9 0.6 copy.15
  107.5 0.0 copy-done
  107.5 0.6 copy.16
Async XLA Ops:
  103.7 3.3 %copy-start.1 = (f32[1536]{0:T(1024)S(1)}, f32[1536]{0:T(1024)}, u32[]{:S(2)}) copy-start(f32[1536]{0:T(1024)} %get-tuple-element.17) | copy-start | bytes 18436
  103.7 3.8 %copy-start = (f32[1536]{0:T(1024)S(1)}, f32[1536]{0:T(1024)}, u32[]{:S(2)}) copy-start(f32[1536]{0:T(1024)} %get-tuple-element.18) | copy-start | bytes 18436
